TPU v7x, 256 devices: a whole 4x4x8 slice. The times are simulated.
256 devices in a mesh: seq: 32 (over x, y, core), dp: 8 (over z).
Axes of the slice: x: 4, y: 4, z: 8, core: 2. Of those that a mesh axis runs over, the one named last changes fastest.
Arguments:
- queries: bfloat16 [65536, 2048], P(('dp', 'seq')), parts along dimension 0, may hold values from -6 to 6
- keys: bfloat16 [65536, 2048], P(('dp', 'seq')), parts along dimension 0, may hold values from -6 to 6
- values: bfloat16 [65536, 2048], P(('dp', 'seq')), parts along dimension 0, may hold values from -6 to 6
- out_grad: bfloat16 [65536, 2048], P(('dp', 'seq')), parts along dimension 0, may hold values from -6 to 6
Outputs:
- attended: bfloat16 [65536, 2048], P(('dp', 'seq')), parts along dimension 0
- grad_query: bfloat16 [65536, 2048], P(('dp', 'seq')), parts along dimension 0
- grad_key: bfloat16 [65536, 2048], P(('dp', 'seq')), parts along dimension 0
- grad_value: bfloat16 [65536, 2048], P(('dp', 'seq')), parts along dimension 0
There are 8 independent parts, one for each index of `dp`. A program takes and returns all parts, laid end to end along the dimension named above; each array names one. Nothing has to cross between parts.
All inputs are finite; a program needn't handle non-finite values.
Results may differ from a plain program's by a relative error of at most 0.0049.
Values sent between devices are 32-bit elements; how exact they have to be, the bound alone decides.
No kernel may reach another device: no remote copies, remote signals or barrier semaphores. Data moves between devices by JAX's collectives and lax.ppermute only.
A program may use at most 256 MiB of HBM per device.

v0:
```python
import functools

import jax
import jax.numpy as jnp
from jax import lax
from jax.experimental import pallas as pl
from jax.experimental.pallas import tpu as pltpu
from jax.sharding import PartitionSpec as P

DH = 128
F32 = jnp.float32
BF16 = jnp.bfloat16
LEFT = (((0,), (0,)), ((), ()))
RIGHT = (((1,), (1,)), ((), ()))
PLAIN = (((1,), (0,)), ((), ()))
MIB = 1024 * 1024
SIDE = 4
PAIR = 2
COLS = PAIR * DH
Q, G, K, V = range(4)
HOPS = (1, 3, 2)

VMEM = pl.BlockSpec(memory_space=pltpu.VMEM)
HBM = pl.BlockSpec(memory_space=pltpu.HBM)
ANY = pl.BlockSpec(memory_space=pl.ANY)


def dot(a, b, dims):
    return lax.dot_general(a, b, dims, preferred_element_type=F32)


def call(body, out_shape, in_specs, out_specs, scratch=(), flops=0, nbytes=0, name=None, limit=8, **kw):
    return pl.pallas_call(
        body,
        in_specs=in_specs,
        out_specs=out_specs,
        out_shape=out_shape,
        scratch_shapes=list(scratch),
        compiler_params=pltpu.CompilerParams(vmem_limit_bytes=limit * MIB),
        cost_estimate=pl.CostEstimate(flops=flops, bytes_accessed=nbytes, transcendentals=0),
        name=name,
        **kw,
    )


def hbm(x):
    return pltpu.with_memory_space_constraint(x, pltpu.HBM)


def aligned(i, size):
    return pl.ds(pl.multiple_of(i * size, size), size)


def ring(i):
    return lax.rem(i + 2 * SIDE, SIDE)


def position():
    index = lax.axis_index("seq")
    return lax.rem(index, 2), lax.div(index, 2 * SIDE), lax.rem(lax.div(index, 2), SIDE)


def own_states(factor, act, out, side, i):
    for j in range(PAIR):
        cols = aligned((side * SIDE + i) * PAIR + j, DH)
        rows = pl.ds(j * DH, DH)
        out[i, 0, rows] = factor * dot(act[K, :, cols], act[V, :, cols], LEFT)
        out[i, 1, rows] = factor * dot(act[Q, :, cols], act[G, :, cols], LEFT)


def send_body(factor, q, g, k, v, out, act, sems):
    mine = position()[0]

    def copies(h, i):
        cols = aligned(h * SIDE + i, COLS)
        return [
            pltpu.make_async_copy(src.at[:, cols], act.at[a, :, cols], sems.at[a, h * SIDE + i])
            for a, src in enumerate((q, g, k, v))
        ]

    for h in (1 - mine, mine):
        for i in range(SIDE):
            for copy in copies(h, i):
                copy.start()

    @pl.loop(0, SIDE)
    def _(i):
        for copy in copies(1 - mine, i):
            copy.wait()
        own_states(factor, act, out, 1 - mine, i)

    for i in range(SIDE):
        for copy in copies(mine, i):
            copy.wait()


def send_states(acts, factor):
    tok, width = acts[0].shape
    return call(
        functools.partial(send_body, factor),
        [jax.ShapeDtypeStruct((SIDE, 2, COLS, DH), F32), jax.ShapeDtypeStruct((4, tok, width), BF16)],
        [HBM] * 4,
        [VMEM] * 2,
        [pltpu.SemaphoreType.DMA((4, width // COLS))],
        flops=2 * width * tok * DH,
        nbytes=8 * tok * width,
        name="send_states",
    )(*map(hbm, acts))


def keep_body(factor, act, out):
    mine = position()[0]
    for i in range(SIDE):
        own_states(factor, act, out, mine, i)


def keep_states(act, factor):
    _, tok, width = act.shape
    return call(
        functools.partial(keep_body, factor),
        jax.ShapeDtypeStruct((SIDE, 2, COLS, DH), F32),
        [VMEM],
        VMEM,
        flops=2 * width * tok * DH,
        nbytes=4 * tok * width,
        name="keep_states",
    )(act)


def chip_body(kept, received, *outs):
    _, _, y = position()
    for d, out in enumerate(outs):
        s = ring(y + d)
        out[...] = kept[s] + received[s]


def chip_states(kept, received):
    return call(
        chip_body,
        [jax.ShapeDtypeStruct(kept.shape[1:], F32)] * SIDE,
        [VMEM] * 2,
        [VMEM] * SIDE,
        flops=kept.size,
        nbytes=kept.size * 12,
        name="chip_states",
    )(kept, received)


def row_body(after, *refs):
    _, x, y = position()
    pieces, (pre, *outs), buf = refs[:SIDE], refs[SIDE:-1], refs[-1]
    for d, piece in zip((0,) + HOPS, pieces):
        buf[ring(y - d)] = piece[...]
    ahead = jnp.zeros(buf.shape[2:], F32)
    behind = ahead
    for s in range(SIDE):
        pre[s, 0] = ahead
        ahead = ahead + buf[s, 0]
    for s in range(SIDE - 1, -1, -1):
        pre[s, 1] = behind
        behind = behind + buf[s, 1]
    for d, out in enumerate(outs, 1):
        out[...] = jnp.where(x + d < SIDE, ahead, behind)


def row_states(after, pieces):
    shape = pieces[0].shape
    return call(
        row_body,
        [jax.ShapeDtypeStruct((SIDE,) + shape, F32)] + [jax.ShapeDtypeStruct(shape[1:], F32)] * (SIDE - 1),
        [ANY] + [VMEM] * SIDE,
        [VMEM] * SIDE,
        [pltpu.VMEM((SIDE,) + shape, F32)],
        flops=8 * pieces[0].size,
        nbytes=40 * pieces[0].size,
        name="row_states",
    )(after, *pieces)


def all_body(pre, *refs):
    _, x, y = position()
    totals, outs = refs[: SIDE - 1], refs[SIDE - 1 :]
    ahead = jnp.zeros(totals[0].shape, F32)
    behind = ahead
    for d, total in zip(HOPS, totals):
        lower = x >= d
        ahead = ahead + jnp.where(lower, total[...], 0.0)
        behind = behind + jnp.where(lower, 0.0, total[...])
    for d, out in enumerate(outs):
        s = ring(y + d)
        out[0] = pre[s, 0] + ahead
        out[1] = pre[s, 1] + behind


def all_states(pre, totals):
    return call(
        all_body,
        [jax.ShapeDtypeStruct(pre.shape[1:], F32)] * SIDE,
        [VMEM] * SIDE,
        [VMEM] * SIDE,
        flops=2 * pre.size,
        nbytes=10 * pre.size,
        name="all_states",
    )(pre, *totals)


def gather_body(after, *refs):
    core, _, y = position()
    pieces, (kept, received, mine, send) = refs[:SIDE], refs[SIDE:]
    second = core.astype(F32)
    first = 1.0 - second
    for d, piece in zip((0,) + HOPS, pieces):
        s = ring(y - d)
        send[s, 0] = piece[0] + first * kept[s, 0]
        send[s, 1] = piece[1] + second * kept[s, 1]
        mine[s, 0] = (piece[0] + second * received[s, 0]).astype(BF16)
        mine[s, 1] = (piece[1] + first * received[s, 1]).astype(BF16)


def gather_states(after, pieces, kept, received):
    return call(
        gather_body,
        [jax.ShapeDtypeStruct(kept.shape, BF16), jax.ShapeDtypeStruct(kept.shape, F32)],
        [ANY] + [VMEM] * (SIDE + 2),
        [VMEM] * 2,
        flops=4 * kept.size,
        nbytes=22 * kept.size,
        name="gather_states",
    )(after, *pieces, kept, received)


def local_body(factor, first, count, after, act, *rest):
    out, tail = rest[-2:]
    tok = act.shape[1]
    causal = lax.broadcasted_iota(jnp.int32, (tok, tok), 0) >= lax.broadcasted_iota(
        jnp.int32, (tok, tok), 1
    )

    @pl.loop(first // PAIR, (first + count) // PAIR)
    def _(i):
        for j in range(PAIR):
            cols = aligned(i * PAIR + j, DH)
            qh, gh, kh, vh = (act[a, :, cols] for a in range(4))
            p = jnp.where(causal, factor * dot(qh, kh, RIGHT), 0.0).astype(BF16)
            e = jnp.where(causal, factor * dot(gh, vh, RIGHT), 0.0).astype(BF16)
            out[Q, :, cols] = dot(p, vh, PLAIN)
            out[G, :, cols] = dot(e, kh, PLAIN)
            out[K, :, cols] = dot(p, gh, LEFT)
            out[V, :, cols] = dot(e, qh, LEFT)

    tail[...] = jnp.zeros(tail.shape, F32)


def local(after, act, factor, first, count, loc=None):
    _, tok, width = act.shape
    args = [after, act]
    aliases = {}
    if loc is not None:
        args.append(loc)
        aliases = {2: 0}
    return call(
        functools.partial(local_body, factor, first, count),
        [jax.ShapeDtypeStruct((4, tok, width), F32), jax.ShapeDtypeStruct((8, DH), F32)],
        [ANY] + [VMEM] * (len(args) - 1),
        [VMEM] * 2,
        flops=12 * tok * tok * DH * count,
        nbytes=tok * width * 12,
        name="local",
        input_output_aliases=aliases,
    )(*args)


def finish_body(own, state, act, loc, *rest):
    outs, (obuf, sems) = rest[-6:-2], rest[-2:]
    core = position()[0]
    side = core if own else 1 - core

    def stores(i):
        return [
            pltpu.make_async_copy(
                obuf.at[a, :, aligned(i, COLS)], out.at[:, aligned(side * SIDE + i, COLS)], sems.at[a, i]
            )
            for a, out in enumerate(outs)
        ]

    @pl.loop(0, SIDE)
    def _(i):
        for j in range(PAIR):
            cols = aligned((side * SIDE + i) * PAIR + j, DH)
            here = aligned(i * PAIR + j, DH)
            rows = pl.ds(j * DH, DH)
            s = state[i, 0, rows].astype(BF16)
            r = state[i, 1, rows].astype(BF16)
            for a, (m, dims) in enumerate(((s, PLAIN), (s, RIGHT), (r, PLAIN), (r, RIGHT))):
                obuf[a, :, here] = (loc[a, :, cols] + dot(act[a, :, cols], m, dims)).astype(BF16)
        for copy in stores(i):
            copy.start()

    for i in range(SIDE):
        for copy in stores(i):
            copy.wait()


def finish(state, act, loc, outs=None):
    _, tok, width = act.shape
    args = [state, act, loc]
    specs = [VMEM] * 3
    aliases = {}
    if outs is not None:
        aliases = {len(args) + i: i for i in range(4)}
        args += map(hbm, outs)
        specs += [HBM] * 4
    return call(
        functools.partial(finish_body, outs is None),
        [pltpu.HBM((tok, width), BF16)] * 4,
        specs,
        [HBM] * 4,
        [pltpu.VMEM((4, tok, width // 2), BF16), pltpu.SemaphoreType.DMA((4, SIDE))],
        flops=4 * tok * DH * width,
        nbytes=tok * width * 16,
        name="finish",
        input_output_aliases=aliases,
    )(*args)


def per_device(q, k, v, g):
    tok, width = q.shape
    heads = width // DH
    n = lax.axis_size("seq")
    factor = float(DH * tok * n) ** (-0.5)
    def to_sibling(t):
        return lax.ppermute(t, "seq", [(i, i ^ 1) for i in range(n)])

    def along_x(t, d):
        return lax.ppermute(t, "seq", [(i, (i + d * 2 * SIDE) % n) for i in range(n)])

    def along_y(t, d):
        row = 2 * SIDE
        return lax.ppermute(t, "seq", [(i, i // row * row + (i + 2 * d) % row) for i in range(n)])

    sent, act = send_states((q, g, k, v), factor)
    received = to_sibling(sent)
    kept = keep_states(act, factor)
    pieces = chip_states(kept, received)
    gathered = [pieces[0]] + [along_y(pieces[d], d) for d in HOPS]
    loc, after = local(pieces[0], act, factor, 0, heads // 2)
    pre, *totals = row_states(after, gathered)
    totals = [along_x(totals[d - 1], d) for d in HOPS]
    pieces = all_states(pre, totals)
    back = [pieces[0]] + [along_y(pieces[d], d) for d in HOPS]
    loc, after = local(pieces[0], act, factor, heads // 2, heads // 2, loc)
    state, send = gather_states(after, back, kept, received)
    got = to_sibling(send)
    outs = finish(state, act, loc)
    o, gq, gv, gk = finish(got, act, loc, outs)
    return o, gq, gk, gv


def solution(mesh):
    placed = P(("dp", "seq"), None)
    return jax.shard_map(
        per_device,
        mesh=mesh,
        in_specs=(placed,) * 4,
        out_specs=(placed,) * 4,
        check_vma=False,
    )
```

profile of v0, /device:TPU:1, one launch (start us, length us, event | category | flops | bytes accessed | tf_op | source)
XLA Modules:
  0.0 53.4 jit_solution(8452993231872250132)
XLA Ops:
  0.6 2.7 %send_states.1 = (f32[4,2,256,128]{3,2,1,0:T(8,128)S(1)}, bf16[4,256,2048]{2,1,0:T(8,128)(2,1)S(1)}) custom-call(bf16[256,2048]{1,0:T(8,128)(2,1)} %q.1, bf16[256,2048]{1,0:T(8,128)(2,1)} %g.1, bf16[256,2048]{1,0:T(8,128)(2,1)} %k.1, bf16[256,2048]{1,0:T(8,128)(2,1)} %v.1), custom_call_target="tpu_custom_call" | custom-call | flops 134217728 | bytes 4194304 | tf_op jit(solution)/shard_map/send_states/pallas_call | solution.py:99
  3.4 3.3 %collective-permute-start = (f32[4,2,256,128]{3,2,1,0:T(8,128)S(1)}, f32[4,2,256,128]{3,2,1,0:T(8,128)S(1)}, u32[]{:S(2)}, u32[]{:S(2)}) collective-permute-start(f32[4,2,256,128]{3,2,1,0:T(8,128)S(1)} %get-tuple-element.33), channel_id=1, source_target_pairs={{0,8},{8,0},{16,24},{24,16},{32,40},{40,32},{48,56},{56,48},{64,72... | collective-permute-start | bytes 3145736 | tf_op jit(solution)/shard_map/ppermute | solution.py:332
  6.7 0.8 %keep_states.1.kept.refs_4_ = f32[4,2,256,128]{3,2,1,0:T(8,128)S(1)} custom-call(bf16[4,256,2048]{2,1,0:T(8,128)(2,1)S(1)} %get-tuple-element.32.act), custom_call_target="tpu_custom_call" | custom-call | flops 134217728 | bytes 2097152 | tf_op jit(solution)/shard_map/keep_states/pallas_call | solution.py:119
  7.5 1.5 %collective-permute-done.received.refs_5_ = f32[4,2,256,128]{3,2,1,0:T(8,128)S(1)} collective-permute-done((f32[4,2,256,128]{3,2,1,0:T(8,128)S(1)}, f32[4,2,256,128]{3,2,1,0:T(8,128)S(1)}, u32[]{:S(2)}, u32[]{:S(2)}) %collective-permute-start) | collective-permute-done | bytes 1048608 | tf_op jit(solution)/shard_map/ppermute | solution.py:332
  9.0 0.1 chip_states.1
  9.1 0.1 collective-permute-start.1
  9.2 2.7 %collective-permute-start.2 = (f32[2,256,128]{2,1,0:T(8,128)S(1)}, f32[2,256,128]{2,1,0:T(8,128)S(1)}, u32[]{:S(2)}, u32[]{:S(2)}) collective-permute-start(f32[2,256,128]{2,1,0:T(8,128)S(1)} %get-tuple-element.37), channel_id=1, source_target_pairs={{0,48},{8,56},{16,0},{24,8},{32,16},{40,24},{48,32},{56,40},{64,11... | collective-permute-start | bytes 786440 | tf_op jit(solution)/shard_map/ppermute | solution.py:339
  11.9 0.0 collective-permute-start.3
  11.9 3.5 %local.2 = (f32[4,256,2048]{2,1,0:T(8,128)S(1)}, f32[8,128]{1,0:T(8,128)S(1)}) custom-call(f32[2,256,128]{2,1,0:T(8,128)S(1)} %get-tuple-element.34.after.refs_0_, bf16[4,256,2048]{2,1,0:T(8,128)(2,1)S(1)} %get-tuple-element.32.act), custom_call_target="tpu_custom_call" | custom-call | flops 805306368 | bytes 6291456 | tf_op jit(solution)/shard_map/local/pallas_call | solution.py:261
  15.4 3.0 %collective-permute-done.1.refs_1_ = f32[2,256,128]{2,1,0:T(8,128)S(1)} collective-permute-done((f32[2,256,128]{2,1,0:T(8,128)S(1)}, f32[2,256,128]{2,1,0:T(8,128)S(1)}, u32[]{:S(2)}, u32[]{:S(2)}) %collective-permute-start.1) | collective-permute-done | bytes 262176 | tf_op jit(solution)/shard_map/ppermute | solution.py:339
  18.4 0.0 collective-permute-done.2.refs_2_
  18.4 4.7 %collective-permute-done.3.refs_3_ = f32[2,256,128]{2,1,0:T(8,128)S(1)} collective-permute-done((f32[2,256,128]{2,1,0:T(8,128)S(1)}, f32[2,256,128]{2,1,0:T(8,128)S(1)}, u32[]{:S(2)}, u32[]{:S(2)}) %collective-permute-start.3) | collective-permute-done | bytes 262176 | tf_op jit(solution)/shard_map/ppermute | solution.py:339
  23.1 0.2 row_states.1
  23.3 1.2 %collective-permute-start.4 = (f32[256,128]{1,0:T(8,128)S(1)}, f32[256,128]{1,0:T(8,128)S(1)}, u32[]{:S(2)}, u32[]{:S(2)}) collective-permute-start(f32[256,128]{1,0:T(8,128)S(1)} %get-tuple-element.40), channel_id=1, source_target_pairs={{0,64},{8,72},{16,80},{24,88},{32,96},{40,104},{48,112},{56,120},{... | collective-permute-start | bytes 393224 | tf_op jit(solution)/shard_map/ppermute | solution.py:335
  24.5 1.5 %collective-permute-start.5 = (f32[256,128]{1,0:T(8,128)S(1)}, f32[256,128]{1,0:T(8,128)S(1)}, u32[]{:S(2)}, u32[]{:S(2)}) collective-permute-start(f32[256,128]{1,0:T(8,128)S(1)} %get-tuple-element.41), channel_id=1, source_target_pairs={{0,192},{8,200},{16,208},{24,216},{32,224},{40,232},{48,240},{56,2... | collective-permute-start | bytes 393224 | tf_op jit(solution)/shard_map/ppermute | solution.py:335
  26.0 1.5 %collective-permute-start.6 = (f32[256,128]{1,0:T(8,128)S(1)}, f32[256,128]{1,0:T(8,128)S(1)}, u32[]{:S(2)}, u32[]{:S(2)}) collective-permute-start(f32[256,128]{1,0:T(8,128)S(1)} %get-tuple-element.42), channel_id=1, source_target_pairs={{0,128},{8,136},{16,144},{24,152},{32,160},{40,168},{48,176},{56,1... | collective-permute-start | bytes 393224 | tf_op jit(solution)/shard_map/ppermute | solution.py:335
  27.5 0.9 %collective-permute-done.4.refs_0_ = f32[256,128]{1,0:T(8,128)S(1)} collective-permute-done((f32[256,128]{1,0:T(8,128)S(1)}, f32[256,128]{1,0:T(8,128)S(1)}, u32[]{:S(2)}, u32[]{:S(2)}) %collective-permute-start.4) | collective-permute-done | bytes 131104 | tf_op jit(solution)/shard_map/ppermute | solution.py:335
  28.4 0.0 collective-permute-done.5.refs_1_
  28.4 4.0 %collective-permute-done.6.refs_2_ = f32[256,128]{1,0:T(8,128)S(1)} collective-permute-done((f32[256,128]{1,0:T(8,128)S(1)}, f32[256,128]{1,0:T(8,128)S(1)}, u32[]{:S(2)}, u32[]{:S(2)}) %collective-permute-start.6) | collective-permute-done | bytes 131104 | tf_op jit(solution)/shard_map/ppermute | solution.py:335
  32.4 0.1 all_states.1
  32.5 0.9 %collective-permute-start.7 = (f32[2,256,128]{2,1,0:T(8,128)S(1)}, f32[2,256,128]{2,1,0:T(8,128)S(1)}, u32[]{:S(2)}, u32[]{:S(2)}) collective-permute-start(f32[2,256,128]{2,1,0:T(8,128)S(1)} %get-tuple-element.46), channel_id=1, source_target_pairs={{0,16},{8,24},{16,32},{24,40},{32,48},{40,56},{48,0},{56,8},{64,80... | collective-permute-start | bytes 786440 | tf_op jit(solution)/shard_map/ppermute | solution.py:339
  33.5 1.8 %collective-permute-start.8 = (f32[2,256,128]{2,1,0:T(8,128)S(1)}, f32[2,256,128]{2,1,0:T(8,128)S(1)}, u32[]{:S(2)}, u32[]{:S(2)}) collective-permute-start(f32[2,256,128]{2,1,0:T(8,128)S(1)} %get-tuple-element.47), channel_id=1, source_target_pairs={{0,48},{8,56},{16,0},{24,8},{32,16},{40,24},{48,32},{56,40},{64,11... | collective-permute-start | bytes 786440 | tf_op jit(solution)/shard_map/ppermute | solution.py:339
  35.3 0.4 collective-permute-start.9
  35.7 3.5 %local.3 = (f32[4,256,2048]{2,1,0:T(8,128)S(1)}, f32[8,128]{1,0:T(8,128)S(1)}) custom-call(f32[2,256,128]{2,1,0:T(8,128)S(1)} %get-tuple-element.43.after.refs_0_, bf16[4,256,2048]{2,1,0:T(8,128)(2,1)S(1)} %get-tuple-element.32.act, f32[4,256,2048]{2,1,0:T(8,128)S(1)} %get-tuple-element.44.rest_0_), custom_call_target="tpu_custom_call", output_to_operand_aliasing={{0}: (2, {})} | custom-call | flops 805306368 | bytes 6291456 | tf_op jit(solution)/shard_map/local/pallas_call | solution.py:261
  39.2 0.0 collective-permute-done.7.refs_1_
  39.2 0.0 collective-permute-done.8.refs_2_
  39.2 5.0 %collective-permute-done.9.refs_3_ = f32[2,256,128]{2,1,0:T(8,128)S(1)} collective-permute-done((f32[2,256,128]{2,1,0:T(8,128)S(1)}, f32[2,256,128]{2,1,0:T(8,128)S(1)}, u32[]{:S(2)}, u32[]{:S(2)}) %collective-permute-start.9) | collective-permute-done | bytes 262176 | tf_op jit(solution)/shard_map/ppermute | solution.py:339
  44.2 0.2 gather_states.1
  44.4 4.4 %collective-permute-start.10 = (f32[4,2,256,128]{3,2,1,0:T(8,128)S(1)}, f32[4,2,256,128]{3,2,1,0:T(8,128)S(1)}, u32[]{:S(2)}, u32[]{:S(2)}) collective-permute-start(f32[4,2,256,128]{3,2,1,0:T(8,128)S(1)} %get-tuple-element.49), channel_id=1, source_target_pairs={{0,8},{8,0},{16,24},{24,16},{32,40},{40,32},{48,56},{56,48},{64,72... | collective-permute-start | bytes 3145736 | tf_op jit(solution)/shard_map/ppermute | solution.py:332
  48.9 2.2 %finish.2 = (bf16[256,2048]{1,0:T(8,128)(2,1)}, bf16[256,2048]{1,0:T(8,128)(2,1)}, bf16[256,2048]{1,0:T(8,128)(2,1)}, bf16[256,2048]{1,0:T(8,128)(2,1)}) custom-call(bf16[4,2,256,128]{3,2,1,0:T(8,128)(2,1)S(1)} %get-tuple-element.51.state, bf16[4,256,2048]{2,1,0:T(8,128)(2,1)S(1)} %get-tuple-element.32.act, f32[4,256,2048]{2,1,0:T(8,128)S(1)} %get-tuple-element.50.loc), custom_call_target="tpu_custom_call" | custom-call | flops 268435456 | bytes 8388608 | tf_op jit(solution)/shard_map/finish/pallas_call | solution.py:313
  51.1 0.1 collective-permute-done.10.state
  51.2 2.2 %finish.3 = (bf16[256,2048]{1,0:T(8,128)(2,1)}, bf16[256,2048]{1,0:T(8,128)(2,1)}, bf16[256,2048]{1,0:T(8,128)(2,1)}, bf16[256,2048]{1,0:T(8,128)(2,1)}) custom-call(f32[4,2,256,128]{3,2,1,0:T(8,128)S(1)} %collective-permute-done.10.state, ...), custom_call_target="tpu_custom_call", output_to_operand_aliasing={{0}: (3, {}), {1}: (4, {}), {2}: (5, {}), {3}: (6, {})} | custom-call | flops 268435456 | bytes 8388608 | tf_op jit(solution)/shard_map/finish/pallas_call | solution.py:313
Async XLA Ops:
  3.4 5.6 %collective-permute-start = (f32[4,2,256,128]{3,2,1,0:T(8,128)S(1)}, f32[4,2,256,128]{3,2,1,0:T(8,128)S(1)}, u32[]{:S(2)}, u32[]{:S(2)}) collective-permute-start(f32[4,2,256,128]{3,2,1,0:T(8,128)S(1)} %get-tuple-element.33), channel_id=1, source_target_pairs={{0,8},{8,0},{16,24},{24,16},{32,40},{40,32},{48,56},{56,48},{64,72... | collective-permute-start | bytes 3145736 | tf_op jit(solution)/shard_map/ppermute | solution.py:332
  9.1 9.3 %collective-permute-start.1 = (f32[2,256,128]{2,1,0:T(8,128)S(1)}, f32[2,256,128]{2,1,0:T(8,128)S(1)}, u32[]{:S(2)}, u32[]{:S(2)}) collective-permute-start(f32[2,256,128]{2,1,0:T(8,128)S(1)} %get-tuple-element.36), channel_id=1, source_target_pairs={{0,16},{8,24},{16,32},{24,40},{32,48},{40,56},{48,0},{56,8},{64,80... | collective-permute-start | bytes 786440 | tf_op jit(solution)/shard_map/ppermute | solution.py:339
  9.2 9.2 %collective-permute-start.2 = (f32[2,256,128]{2,1,0:T(8,128)S(1)}, f32[2,256,128]{2,1,0:T(8,128)S(1)}, u32[]{:S(2)}, u32[]{:S(2)}) collective-permute-start(f32[2,256,128]{2,1,0:T(8,128)S(1)} %get-tuple-element.37), channel_id=1, source_target_pairs={{0,48},{8,56},{16,0},{24,8},{32,16},{40,24},{48,32},{56,40},{64,11... | collective-permute-start | bytes 786440 | tf_op jit(solution)/shard_map/ppermute | solution.py:339
  11.9 11.2 %collective-permute-start.3 = (f32[2,256,128]{2,1,0:T(8,128)S(1)}, f32[2,256,128]{2,1,0:T(8,128)S(1)}, u32[]{:S(2)}, u32[]{:S(2)}) collective-permute-start(f32[2,256,128]{2,1,0:T(8,128)S(1)} %get-tuple-element.38), channel_id=1, source_target_pairs={{0,32},{8,40},{16,48},{24,56},{32,0},{40,8},{48,16},{56,24},{64,96... | collective-permute-start | bytes 786440 | tf_op jit(solution)/shard_map/ppermute | solution.py:339
  23.3 5.1 %collective-permute-start.4 = (f32[256,128]{1,0:T(8,128)S(1)}, f32[256,128]{1,0:T(8,128)S(1)}, u32[]{:S(2)}, u32[]{:S(2)}) collective-permute-start(f32[256,128]{1,0:T(8,128)S(1)} %get-tuple-element.40), channel_id=1, source_target_pairs={{0,64},{8,72},{16,80},{24,88},{32,96},{40,104},{48,112},{56,120},{... | collective-permute-start | bytes 393224 | tf_op jit(solution)/shard_map/ppermute | solution.py:335
  24.5 3.9 %collective-permute-start.5 = (f32[256,128]{1,0:T(8,128)S(1)}, f32[256,128]{1,0:T(8,128)S(1)}, u32[]{:S(2)}, u32[]{:S(2)}) collective-permute-start(f32[256,128]{1,0:T(8,128)S(1)} %get-tuple-element.41), channel_id=1, source_target_pairs={{0,192},{8,200},{16,208},{24,216},{32,224},{40,232},{48,240},{56,2... | collective-permute-start | bytes 393224 | tf_op jit(solution)/shard_map/ppermute | solution.py:335
  26.0 6.4 %collective-permute-start.6 = (f32[256,128]{1,0:T(8,128)S(1)}, f32[256,128]{1,0:T(8,128)S(1)}, u32[]{:S(2)}, u32[]{:S(2)}) collective-permute-start(f32[256,128]{1,0:T(8,128)S(1)} %get-tuple-element.42), channel_id=1, source_target_pairs={{0,128},{8,136},{16,144},{24,152},{32,160},{40,168},{48,176},{56,1... | collective-permute-start | bytes 393224 | tf_op jit(solution)/shard_map/ppermute | solution.py:335
  32.5 6.6 %collective-permute-start.7 = (f32[2,256,128]{2,1,0:T(8,128)S(1)}, f32[2,256,128]{2,1,0:T(8,128)S(1)}, u32[]{:S(2)}, u32[]{:S(2)}) collective-permute-start(f32[2,256,128]{2,1,0:T(8,128)S(1)} %get-tuple-element.46), channel_id=1, source_target_pairs={{0,16},{8,24},{16,32},{24,40},{32,48},{40,56},{48,0},{56,8},{64,80... | collective-permute-start | bytes 786440 | tf_op jit(solution)/shard_map/ppermute | solution.py:339
  33.5 5.7 %collective-permute-start.8 = (f32[2,256,128]{2,1,0:T(8,128)S(1)}, f32[2,256,128]{2,1,0:T(8,128)S(1)}, u32[]{:S(2)}, u32[]{:S(2)}) collective-permute-start(f32[2,256,128]{2,1,0:T(8,128)S(1)} %get-tuple-element.47), channel_id=1, source_target_pairs={{0,48},{8,56},{16,0},{24,8},{32,16},{40,24},{48,32},{56,40},{64,11... | collective-permute-start | bytes 786440 | tf_op jit(solution)/shard_map/ppermute | solution.py:339
  35.3 8.9 %collective-permute-start.9 = (f32[2,256,128]{2,1,0:T(8,128)S(1)}, f32[2,256,128]{2,1,0:T(8,128)S(1)}, u32[]{:S(2)}, u32[]{:S(2)}) collective-permute-start(f32[2,256,128]{2,1,0:T(8,128)S(1)} %get-tuple-element.48), channel_id=1, source_target_pairs={{0,32},{8,40},{16,48},{24,56},{32,0},{40,8},{48,16},{56,24},{64,96... | collective-permute-start | bytes 786440 | tf_op jit(solution)/shard_map/ppermute | solution.py:339
  44.4 6.7 %collective-permute-start.10 = (f32[4,2,256,128]{3,2,1,0:T(8,128)S(1)}, f32[4,2,256,128]{3,2,1,0:T(8,128)S(1)}, u32[]{:S(2)}, u32[]{:S(2)}) collective-permute-start(f32[4,2,256,128]{3,2,1,0:T(8,128)S(1)} %get-tuple-element.49), channel_id=1, source_target_pairs={{0,8},{8,0},{16,24},{24,16},{32,40},{40,32},{48,56},{56,48},{64,72... | collective-permute-start | bytes 3145736 | tf_op jit(solution)/shard_map/ppermute | solution.py:332
where the time goes:
time: 53.5 us; the launch traced here: 53.4 us
  waiting for transfers between devices  19.1 us (36%)
  starting transfers between devices  17.9 us (33%)
  Pallas kernels  15.7 us (29%)
  between operations  0.71 us (1%)
    ppermute x6, waiting for transfers between devices, along_y(): lax.ppermute(t, 'seq', [(i, i // row * row + (i + 2 * d) % row) for i in...  12.7 us
    ppermute x2, starting transfers between devices, to_sibling(): return lax.ppermute(t, 'seq', [(i, i ^ 1) for i in range(n)])  7.76 us
    pallas_call x2, Pallas kernels, local(): call(functools.partial(local_body, factor, first, count), [jax.ShapeDtype...  6.98 us
    ppermute x6, starting transfers between devices, along_y(): lax.ppermute(t, 'seq', [(i, i // row * row + (i + 2 * d) % row) for i in...  5.89 us
    ppermute x3, waiting for transfers between devices, along_x(): lax.ppermute(t, 'seq', [(i, (i + d * 2 * SIDE) % n) for i in range(n)])  4.87 us
    pallas_call x2, Pallas kernels, finish(): call(functools.partial(finish_body, outs is None), [pltpu.HBM((tok, width...  4.47 us
    ppermute x3, starting transfers between devices, along_x(): lax.ppermute(t, 'seq', [(i, (i + d * 2 * SIDE) % n) for i in range(n)])  4.25 us
    pallas_call x1, Pallas kernels, send_states(): call(functools.partial(send_body, factor), [jax.ShapeDtypeStruct((SIDE, 2...  2.73 us
  transfers between devices with their start and end apart: 11, of which 7 were waited for; matrix products, arithmetic and copies ran while one was open for 0% of the time, Pallas kernels for 19%

commit v1 on v0

--- a/solution.py
+++ b/solution.py
@@ -19,6 +19,8 @@
 COLS = PAIR * DH
 Q, G, K, V = range(4)
 HOPS = (1, 3, 2)
+ORDER = HOPS + (0,)
+EARLY = 2
 
 VMEM = pl.BlockSpec(memory_space=pltpu.VMEM)
 HBM = pl.BlockSpec(memory_space=pltpu.HBM)
@@ -60,16 +62,16 @@
     return lax.rem(index, 2), lax.div(index, 2 * SIDE), lax.rem(lax.div(index, 2), SIDE)
 
 
-def own_states(factor, act, out, side, i):
+def own_states(factor, act, out, slot, side, i):
     for j in range(PAIR):
         cols = aligned((side * SIDE + i) * PAIR + j, DH)
         rows = pl.ds(j * DH, DH)
-        out[i, 0, rows] = factor * dot(act[K, :, cols], act[V, :, cols], LEFT)
-        out[i, 1, rows] = factor * dot(act[Q, :, cols], act[G, :, cols], LEFT)
-
-
-def send_body(factor, q, g, k, v, out, act, sems):
-    mine = position()[0]
+        out[slot, 0, rows] = factor * dot(act[K, :, cols], act[V, :, cols], LEFT)
+        out[slot, 1, rows] = factor * dot(act[Q, :, cols], act[G, :, cols], LEFT)
+
+
+def send_body(factor, q, g, k, v, early, late, act, sems):
+    mine, _, y = position()
 
     def copies(h, i):
         cols = aligned(h * SIDE + i, COLS)
@@ -79,15 +81,15 @@
         ]
 
     for h in (1 - mine, mine):
-        for i in range(SIDE):
-            for copy in copies(h, i):
+        for d in ORDER:
+            for copy in copies(h, ring(y + d)):
                 copy.start()
-
-    @pl.loop(0, SIDE)
-    def _(i):
+    for slot, d in enumerate(ORDER):
+        i = ring(y + d)
         for copy in copies(1 - mine, i):
             copy.wait()
-        own_states(factor, act, out, 1 - mine, i)
+        out = early if slot < EARLY else late
+        own_states(factor, act, out, slot % EARLY, 1 - mine, i)
 
     for i in range(SIDE):
         for copy in copies(mine, i):
@@ -98,9 +100,9 @@
     tok, width = acts[0].shape
     return call(
         functools.partial(send_body, factor),
-        [jax.ShapeDtypeStruct((SIDE, 2, COLS, DH), F32), jax.ShapeDtypeStruct((4, tok, width), BF16)],
+        [jax.ShapeDtypeStruct((EARLY, 2, COLS, DH), F32)] * 2 + [jax.ShapeDtypeStruct((4, tok, width), BF16)],
         [HBM] * 4,
-        [VMEM] * 2,
+        [VMEM] * 3,
         [pltpu.SemaphoreType.DMA((4, width // COLS))],
         flops=2 * width * tok * DH,
         nbytes=8 * tok * width,
@@ -109,9 +111,9 @@
 
 
 def keep_body(factor, act, out):
-    mine = position()[0]
-    for i in range(SIDE):
-        own_states(factor, act, out, mine, i)
+    mine, _, y = position()
+    for slot, d in enumerate(ORDER):
+        own_states(factor, act, out, slot, mine, ring(y + d))
 
 
 def keep_states(act, factor):
@@ -127,21 +129,19 @@
     )(act)
 
 
-def chip_body(kept, received, *outs):
-    _, _, y = position()
-    for d, out in enumerate(outs):
-        s = ring(y + d)
-        out[...] = kept[s] + received[s]
-
-
-def chip_states(kept, received):
-    return call(
-        chip_body,
-        [jax.ShapeDtypeStruct(kept.shape[1:], F32)] * SIDE,
+def chip_body(first, kept, received, *outs):
+    for i, out in enumerate(outs):
+        out[...] = kept[first + i] + received[i]
+
+
+def chip_states(first, kept, received):
+    return call(
+        functools.partial(chip_body, first),
+        [jax.ShapeDtypeStruct(kept.shape[1:], F32)] * EARLY,
         [VMEM] * 2,
-        [VMEM] * SIDE,
-        flops=kept.size,
-        nbytes=kept.size * 12,
+        [VMEM] * EARLY,
+        flops=received.size,
+        nbytes=received.size * 12,
         name="chip_states",
     )(kept, received)
 
@@ -206,27 +206,29 @@
 
 def gather_body(after, *refs):
     core, _, y = position()
-    pieces, (kept, received, mine, send) = refs[:SIDE], refs[SIDE:]
+    pieces, (kept, early, late, mine, send) = refs[:SIDE], refs[SIDE:]
     second = core.astype(F32)
     first = 1.0 - second
     for d, piece in zip((0,) + HOPS, pieces):
         s = ring(y - d)
-        send[s, 0] = piece[0] + first * kept[s, 0]
-        send[s, 1] = piece[1] + second * kept[s, 1]
-        mine[s, 0] = (piece[0] + second * received[s, 0]).astype(BF16)
-        mine[s, 1] = (piece[1] + first * received[s, 1]).astype(BF16)
+        slot = ORDER.index((SIDE - d) % SIDE)
+        received = (early if slot < EARLY else late).at[slot % EARLY]
+        send[s, 0] = piece[0] + first * kept[slot, 0]
+        send[s, 1] = piece[1] + second * kept[slot, 1]
+        mine[s, 0] = (piece[0] + second * received[0]).astype(BF16)
+        mine[s, 1] = (piece[1] + first * received[1]).astype(BF16)
 
 
 def gather_states(after, pieces, kept, received):
     return call(
         gather_body,
         [jax.ShapeDtypeStruct(kept.shape, BF16), jax.ShapeDtypeStruct(kept.shape, F32)],
-        [ANY] + [VMEM] * (SIDE + 2),
+        [ANY] + [VMEM] * (SIDE + 3),
         [VMEM] * 2,
         flops=4 * kept.size,
         nbytes=22 * kept.size,
         name="gather_states",
-    )(after, *pieces, kept, received)
+    )(after, *pieces, kept, *received)
 
 
 def local_body(factor, first, count, after, act, *rest):
@@ -338,10 +340,11 @@
         row = 2 * SIDE
         return lax.ppermute(t, "seq", [(i, i // row * row + (i + 2 * d) % row) for i in range(n)])
 
-    sent, act = send_states((q, g, k, v), factor)
-    received = to_sibling(sent)
+    *sent, act = send_states((q, g, k, v), factor)
+    received = [to_sibling(t) for t in sent]
     kept = keep_states(act, factor)
-    pieces = chip_states(kept, received)
+    pieces = [t for i in range(2) for t in chip_states(i * EARLY, kept, received[i])]
+    pieces = dict(zip(ORDER, pieces))
     gathered = [pieces[0]] + [along_y(pieces[d], d) for d in HOPS]
     loc, after = local(pieces[0], act, factor, 0, heads // 2)
     pre, *totals = row_states(after, gathered)

time: 53.5 us -> 52.7 us (0.985)
  waiting for transfers between devices: 19.1 us -> 18.1 us
    ppermute x2 -> x3, waiting for transfers between devices: 1.52 us -> 0.65 us  [to_sibling(): return lax.ppermute(t, 'seq', [(i, i ^ 1) for i in range(n)])]
    ppermute x2 -> x3, starting transfers between devices: 7.76 us -> 7.86 us  [to_sibling(): return lax.ppermute(t, 'seq', [(i, i ^ 1) for i in range(n)])]
    pallas_call x2 -> x3, Pallas kernels: 2.84 us -> 2.85 us  [the longest x1 2.74 us: send_states(): call(functools.partial(send_body, factor), [jax.ShapeDtypeStruct((EARLY,...]
  transfers between devices with their start and end apart: 11 -> 12, of which waited for: 7 -> 6; matrix products, arithmetic and copies ran while one was open for 0% -> 0% of each run, Pallas kernels for 19% -> 19%
where the time goes in v1:
time: 52.7 us; the launch traced here: 52.6 us
  starting transfers between devices  18.1 us (34%)
  waiting for transfers between devices  18.1 us (34%)
  Pallas kernels  15.7 us (30%)
  between operations  0.72 us (1%)
    ppermute x6, waiting for transfers between devices, along_y(): lax.ppermute(t, 'seq', [(i, i // row * row + (i + 2 * d) % row) for i in...  12.6 us
    ppermute x3, starting transfers between devices, to_sibling(): return lax.ppermute(t, 'seq', [(i, i ^ 1) for i in range(n)])  7.86 us
    pallas_call x2, Pallas kernels, local(): call(functools.partial(local_body, factor, first, count), [jax.ShapeDtype...  6.97 us
    ppermute x6, starting transfers between devices, along_y(): lax.ppermute(t, 'seq', [(i, i // row * row + (i + 2 * d) % row) for i in...  5.98 us
    ppermute x3, waiting for transfers between devices, along_x(): lax.ppermute(t, 'seq', [(i, (i + d * 2 * SIDE) % n) for i in range(n)])  4.87 us
    pallas_call x2, Pallas kernels, finish(): call(functools.partial(finish_body, outs is None), [pltpu.HBM((tok, width...  4.49 us
    ppermute x3, starting transfers between devices, along_x(): lax.ppermute(t, 'seq', [(i, (i + d * 2 * SIDE) % n) for i in range(n)])  4.25 us
    pallas_call x1, Pallas kernels, send_states(): call(functools.partial(send_body, factor), [jax.ShapeDtypeStruct((EARLY,...  2.74 us
  transfers between devices with their start and end apart: 12, of which 6 were waited for; matrix products, arithmetic and copies ran while one was open for 0% of the time, Pallas kernels for 19%

profile of v1, /device:TPU:1, one launch (start us, length us, event | category | flops | bytes accessed | tf_op | source)
XLA Modules:
  0.0 52.6 jit_solution(3394433834019125974)
XLA Ops:
  0.6 2.7 %send_states.1 = (f32[2,2,256,128]{3,2,1,0:T(8,128)S(1)}, f32[2,2,256,128]{3,2,1,0:T(8,128)S(1)}, bf16[4,256,2048]{2,1,0:T(8,128)(2,1)S(1)}) custom-call(bf16[256,2048]{1,0:T(8,128)(2,1)} %q.1, bf16[256,2048]{1,0:T(8,128)(2,1)} %g.1, bf16[256,2048]{1,0:T(8,128)(2,1)} %k.1, bf16[256,2048]{1,0:T(8,128)(2,1)} %v.1), custom_call_target="tpu_custom_call" | custom-call | flops 134217728 | bytes 4194304 | tf_op jit(solution)/shard_map/send_states/pallas_call | solution.py:101
  3.4 3.3 %collective-permute-start.1 = (f32[2,2,256,128]{3,2,1,0:T(8,128)S(1)}, f32[2,2,256,128]{3,2,1,0:T(8,128)S(1)}, u32[]{:S(2)}, u32[]{:S(2)}) collective-permute-start(f32[2,2,256,128]{3,2,1,0:T(8,128)S(1)} %get-tuple-element.37), channel_id=1, source_target_pairs={{0,8},{8,0},{16,24},{24,16},{32,40},{40,32},{48,56},{56,48},{64,72... | collective-permute-start | bytes 1572872 | tf_op jit(solution)/shard_map/ppermute | solution.py:334
  6.7 0.1 collective-permute-start
  6.8 0.8 %keep_states.1.kept.refs_4_ = f32[4,2,256,128]{3,2,1,0:T(8,128)S(1)} custom-call(bf16[4,256,2048]{2,1,0:T(8,128)(2,1)S(1)} %get-tuple-element.33.act), custom_call_target="tpu_custom_call" | custom-call | flops 134217728 | bytes 2097152 | tf_op jit(solution)/shard_map/keep_states/pallas_call | solution.py:121
  7.6 0.6 %collective-permute-done.1.received.refs_5_ = f32[2,2,256,128]{3,2,1,0:T(8,128)S(1)} collective-permute-done((f32[2,2,256,128]{3,2,1,0:T(8,128)S(1)}, f32[2,2,256,128]{3,2,1,0:T(8,128)S(1)}, u32[]{:S(2)}, u32[]{:S(2)}) %collective-permute-start.1) | collective-permute-done | bytes 524320 | tf_op jit(solution)/shard_map/ppermute | solution.py:334
  8.2 0.1 chip_states.3
  8.3 0.1 collective-permute-start.2
  8.4 2.7 %collective-permute-start.3 = (f32[2,256,128]{2,1,0:T(8,128)S(1)}, f32[2,256,128]{2,1,0:T(8,128)S(1)}, u32[]{:S(2)}, u32[]{:S(2)}) collective-permute-start(f32[2,256,128]{2,1,0:T(8,128)S(1)} %get-tuple-element.39), channel_id=1, source_target_pairs={{0,48},{8,56},{16,0},{24,8},{32,16},{40,24},{48,32},{56,40},{64,11... | collective-permute-start | bytes 786440 | tf_op jit(solution)/shard_map/ppermute | solution.py:341
  11.1 0.0 collective-permute-done.received.refs_6_
  11.1 0.1 chip_states.2
  11.1 0.1 collective-permute-start.4
  11.2 3.5 %local.2 = (f32[4,256,2048]{2,1,0:T(8,128)S(1)}, f32[8,128]{1,0:T(8,128)S(1)}) custom-call(f32[2,256,128]{2,1,0:T(8,128)S(1)} %get-tuple-element.35.after.refs_0_, bf16[4,256,2048]{2,1,0:T(8,128)(2,1)S(1)} %get-tuple-element.33.act), custom_call_target="tpu_custom_call" | custom-call | flops 805306368 | bytes 6291456 | tf_op jit(solution)/shard_map/local/pallas_call | solution.py:263
  14.7 2.9 %collective-permute-done.2.refs_1_ = f32[2,256,128]{2,1,0:T(8,128)S(1)} collective-permute-done((f32[2,256,128]{2,1,0:T(8,128)S(1)}, f32[2,256,128]{2,1,0:T(8,128)S(1)}, u32[]{:S(2)}, u32[]{:S(2)}) %collective-permute-start.2) | collective-permute-done | bytes 262176 | tf_op jit(solution)/shard_map/ppermute | solution.py:341
  17.6 4.7 %collective-permute-done.4.refs_3_ = f32[2,256,128]{2,1,0:T(8,128)S(1)} collective-permute-done((f32[2,256,128]{2,1,0:T(8,128)S(1)}, f32[2,256,128]{2,1,0:T(8,128)S(1)}, u32[]{:S(2)}, u32[]{:S(2)}) %collective-permute-start.4) | collective-permute-done | bytes 262176 | tf_op jit(solution)/shard_map/ppermute | solution.py:341
  22.3 0.2 row_states.1
  22.5 1.2 %collective-permute-start.5 = (f32[256,128]{1,0:T(8,128)S(1)}, f32[256,128]{1,0:T(8,128)S(1)}, u32[]{:S(2)}, u32[]{:S(2)}) collective-permute-start(f32[256,128]{1,0:T(8,128)S(1)} %get-tuple-element.42), channel_id=1, source_target_pairs={{0,64},{8,72},{16,80},{24,88},{32,96},{40,104},{48,112},{56,120},{... | collective-permute-start | bytes 393224 | tf_op jit(solution)/shard_map/ppermute | solution.py:337
  23.7 1.5 %collective-permute-start.6 = (f32[256,128]{1,0:T(8,128)S(1)}, f32[256,128]{1,0:T(8,128)S(1)}, u32[]{:S(2)}, u32[]{:S(2)}) collective-permute-start(f32[256,128]{1,0:T(8,128)S(1)} %get-tuple-element.43), channel_id=1, source_target_pairs={{0,192},{8,200},{16,208},{24,216},{32,224},{40,232},{48,240},{56,2... | collective-permute-start | bytes 393224 | tf_op jit(solution)/shard_map/ppermute | solution.py:337
  25.2 1.5 %collective-permute-start.7 = (f32[256,128]{1,0:T(8,128)S(1)}, f32[256,128]{1,0:T(8,128)S(1)}, u32[]{:S(2)}, u32[]{:S(2)}) collective-permute-start(f32[256,128]{1,0:T(8,128)S(1)} %get-tuple-element.44), channel_id=1, source_target_pairs={{0,128},{8,136},{16,144},{24,152},{32,160},{40,168},{48,176},{56,1... | collective-permute-start | bytes 393224 | tf_op jit(solution)/shard_map/ppermute | solution.py:337
  26.7 0.9 %collective-permute-done.5.refs_0_ = f32[256,128]{1,0:T(8,128)S(1)} collective-permute-done((f32[256,128]{1,0:T(8,128)S(1)}, f32[256,128]{1,0:T(8,128)S(1)}, u32[]{:S(2)}, u32[]{:S(2)}) %collective-permute-start.5) | collective-permute-done | bytes 131104 | tf_op jit(solution)/shard_map/ppermute | solution.py:337
  27.6 4.0 %collective-permute-done.7.refs_2_ = f32[256,128]{1,0:T(8,128)S(1)} collective-permute-done((f32[256,128]{1,0:T(8,128)S(1)}, f32[256,128]{1,0:T(8,128)S(1)}, u32[]{:S(2)}, u32[]{:S(2)}) %collective-permute-start.7) | collective-permute-done | bytes 131104 | tf_op jit(solution)/shard_map/ppermute | solution.py:337
  31.6 0.1 all_states.1
  31.7 0.9 %collective-permute-start.8 = (f32[2,256,128]{2,1,0:T(8,128)S(1)}, f32[2,256,128]{2,1,0:T(8,128)S(1)}, u32[]{:S(2)}, u32[]{:S(2)}) collective-permute-start(f32[2,256,128]{2,1,0:T(8,128)S(1)} %get-tuple-element.48), channel_id=1, source_target_pairs={{0,16},{8,24},{16,32},{24,40},{32,48},{40,56},{48,0},{56,8},{64,80... | collective-permute-start | bytes 786440 | tf_op jit(solution)/shard_map/ppermute | solution.py:341
  32.7 1.8 %collective-permute-start.9 = (f32[2,256,128]{2,1,0:T(8,128)S(1)}, f32[2,256,128]{2,1,0:T(8,128)S(1)}, u32[]{:S(2)}, u32[]{:S(2)}) collective-permute-start(f32[2,256,128]{2,1,0:T(8,128)S(1)} %get-tuple-element.49), channel_id=1, source_target_pairs={{0,48},{8,56},{16,0},{24,8},{32,16},{40,24},{48,32},{56,40},{64,11... | collective-permute-start | bytes 786440 | tf_op jit(solution)/shard_map/ppermute | solution.py:341
  34.5 0.4 collective-permute-start.10
  34.9 3.5 %local.3 = (f32[4,256,2048]{2,1,0:T(8,128)S(1)}, f32[8,128]{1,0:T(8,128)S(1)}) custom-call(f32[2,256,128]{2,1,0:T(8,128)S(1)} %get-tuple-element.45.after.refs_0_, bf16[4,256,2048]{2,1,0:T(8,128)(2,1)S(1)} %get-tuple-element.33.act, f32[4,256,2048]{2,1,0:T(8,128)S(1)} %get-tuple-element.46.rest_0_), custom_call_target="tpu_custom_call", output_to_operand_aliasing={{0}: (2, {})} | custom-call | flops 805306368 | bytes 6291456 | tf_op jit(solution)/shard_map/local/pallas_call | solution.py:263
  38.4 0.0 collective-permute-done.9.refs_2_
  38.4 5.0 %collective-permute-done.10.refs_3_ = f32[2,256,128]{2,1,0:T(8,128)S(1)} collective-permute-done((f32[2,256,128]{2,1,0:T(8,128)S(1)}, f32[2,256,128]{2,1,0:T(8,128)S(1)}, u32[]{:S(2)}, u32[]{:S(2)}) %collective-permute-start.10) | collective-permute-done | bytes 262176 | tf_op jit(solution)/shard_map/ppermute | solution.py:341
  43.4 0.2 gather_states.1
  43.6 4.4 %collective-permute-start.11 = (f32[4,2,256,128]{3,2,1,0:T(8,128)S(1)}, f32[4,2,256,128]{3,2,1,0:T(8,128)S(1)}, u32[]{:S(2)}, u32[]{:S(2)}) collective-permute-start(f32[4,2,256,128]{3,2,1,0:T(8,128)S(1)} %get-tuple-element.51), channel_id=1, source_target_pairs={{0,8},{8,0},{16,24},{24,16},{32,40},{40,32},{48,56},{56,48},{64,72... | collective-permute-start | bytes 3145736 | tf_op jit(solution)/shard_map/ppermute | solution.py:334
  48.1 2.2 %finish.2 = (bf16[256,2048]{1,0:T(8,128)(2,1)}, bf16[256,2048]{1,0:T(8,128)(2,1)}, bf16[256,2048]{1,0:T(8,128)(2,1)}, bf16[256,2048]{1,0:T(8,128)(2,1)}) custom-call(bf16[4,2,256,128]{3,2,1,0:T(8,128)(2,1)S(1)} %get-tuple-element.53.state, bf16[4,256,2048]{2,1,0:T(8,128)(2,1)S(1)} %get-tuple-element.33.act, f32[4,256,2048]{2,1,0:T(8,128)S(1)} %get-tuple-element.52.loc), custom_call_target="tpu_custom_call" | custom-call | flops 268435456 | bytes 8388608 | tf_op jit(solution)/shard_map/finish/pallas_call | solution.py:315
  50.3 0.0 collective-permute-done.11.state
  50.4 2.2 %finish.3 = (bf16[256,2048]{1,0:T(8,128)(2,1)}, bf16[256,2048]{1,0:T(8,128)(2,1)}, bf16[256,2048]{1,0:T(8,128)(2,1)}, bf16[256,2048]{1,0:T(8,128)(2,1)}) custom-call(f32[4,2,256,128]{3,2,1,0:T(8,128)S(1)} %collective-permute-done.11.state, ...), custom_call_target="tpu_custom_call", output_to_operand_aliasing={{0}: (3, {}), {1}: (4, {}), {2}: (5, {}), {3}: (6, {})} | custom-call | flops 268435456 | bytes 8388608 | tf_op jit(solution)/shard_map/finish/pallas_call | solution.py:315
  (3 shorter events, 0.0 us)
Async XLA Ops:
  3.4 4.9 %collective-permute-start.1 = (f32[2,2,256,128]{3,2,1,0:T(8,128)S(1)}, f32[2,2,256,128]{3,2,1,0:T(8,128)S(1)}, u32[]{:S(2)}, u32[]{:S(2)}) collective-permute-start(f32[2,2,256,128]{3,2,1,0:T(8,128)S(1)} %get-tuple-element.37), channel_id=1, source_target_pairs={{0,8},{8,0},{16,24},{24,16},{32,40},{40,32},{48,56},{56,48},{64,72... | collective-permute-start | bytes 1572872 | tf_op jit(solution)/shard_map/ppermute | solution.py:334
  6.7 4.4 %collective-permute-start = (f32[2,2,256,128]{3,2,1,0:T(8,128)S(1)}, f32[2,2,256,128]{3,2,1,0:T(8,128)S(1)}, u32[]{:S(2)}, u32[]{:S(2)}) collective-permute-start(f32[2,2,256,128]{3,2,1,0:T(8,128)S(1)} %get-tuple-element.34), channel_id=1, source_target_pairs={{0,8},{8,0},{16,24},{24,16},{32,40},{40,32},{48,56},{56,48},{64,72... | collective-permute-start | bytes 1572872 | tf_op jit(solution)/shard_map/ppermute | solution.py:334
  8.3 9.3 %collective-permute-start.2 = (f32[2,256,128]{2,1,0:T(8,128)S(1)}, f32[2,256,128]{2,1,0:T(8,128)S(1)}, u32[]{:S(2)}, u32[]{:S(2)}) collective-permute-start(f32[2,256,128]{2,1,0:T(8,128)S(1)} %get-tuple-element.38), channel_id=1, source_target_pairs={{0,16},{8,24},{16,32},{24,40},{32,48},{40,56},{48,0},{56,8},{64,80... | collective-permute-start | bytes 786440 | tf_op jit(solution)/shard_map/ppermute | solution.py:341
  8.4 9.2 %collective-permute-start.3 = (f32[2,256,128]{2,1,0:T(8,128)S(1)}, f32[2,256,128]{2,1,0:T(8,128)S(1)}, u32[]{:S(2)}, u32[]{:S(2)}) collective-permute-start(f32[2,256,128]{2,1,0:T(8,128)S(1)} %get-tuple-element.39), channel_id=1, source_target_pairs={{0,48},{8,56},{16,0},{24,8},{32,16},{40,24},{48,32},{56,40},{64,11... | collective-permute-start | bytes 786440 | tf_op jit(solution)/shard_map/ppermute | solution.py:341
  11.1 11.2 %collective-permute-start.4 = (f32[2,256,128]{2,1,0:T(8,128)S(1)}, f32[2,256,128]{2,1,0:T(8,128)S(1)}, u32[]{:S(2)}, u32[]{:S(2)}) collective-permute-start(f32[2,256,128]{2,1,0:T(8,128)S(1)} %get-tuple-element.40), channel_id=1, source_target_pairs={{0,32},{8,40},{16,48},{24,56},{32,0},{40,8},{48,16},{56,24},{64,96... | collective-permute-start | bytes 786440 | tf_op jit(solution)/shard_map/ppermute | solution.py:341
  22.5 5.1 %collective-permute-start.5 = (f32[256,128]{1,0:T(8,128)S(1)}, f32[256,128]{1,0:T(8,128)S(1)}, u32[]{:S(2)}, u32[]{:S(2)}) collective-permute-start(f32[256,128]{1,0:T(8,128)S(1)} %get-tuple-element.42), channel_id=1, source_target_pairs={{0,64},{8,72},{16,80},{24,88},{32,96},{40,104},{48,112},{56,120},{... | collective-permute-start | bytes 393224 | tf_op jit(solution)/shard_map/ppermute | solution.py:337
  23.7 3.9 %collective-permute-start.6 = (f32[256,128]{1,0:T(8,128)S(1)}, f32[256,128]{1,0:T(8,128)S(1)}, u32[]{:S(2)}, u32[]{:S(2)}) collective-permute-start(f32[256,128]{1,0:T(8,128)S(1)} %get-tuple-element.43), channel_id=1, source_target_pairs={{0,192},{8,200},{16,208},{24,216},{32,224},{40,232},{48,240},{56,2... | collective-permute-start | bytes 393224 | tf_op jit(solution)/shard_map/ppermute | solution.py:337
  25.2 6.4 %collective-permute-start.7 = (f32[256,128]{1,0:T(8,128)S(1)}, f32[256,128]{1,0:T(8,128)S(1)}, u32[]{:S(2)}, u32[]{:S(2)}) collective-permute-start(f32[256,128]{1,0:T(8,128)S(1)} %get-tuple-element.44), channel_id=1, source_target_pairs={{0,128},{8,136},{16,144},{24,152},{32,160},{40,168},{48,176},{56,1... | collective-permute-start | bytes 393224 | tf_op jit(solution)/shard_map/ppermute | solution.py:337
  31.7 6.6 %collective-permute-start.8 = (f32[2,256,128]{2,1,0:T(8,128)S(1)}, f32[2,256,128]{2,1,0:T(8,128)S(1)}, u32[]{:S(2)}, u32[]{:S(2)}) collective-permute-start(f32[2,256,128]{2,1,0:T(8,128)S(1)} %get-tuple-element.48), channel_id=1, source_target_pairs={{0,16},{8,24},{16,32},{24,40},{32,48},{40,56},{48,0},{56,8},{64,80... | collective-permute-start | bytes 786440 | tf_op jit(solution)/shard_map/ppermute | solution.py:341
  32.7 5.7 %collective-permute-start.9 = (f32[2,256,128]{2,1,0:T(8,128)S(1)}, f32[2,256,128]{2,1,0:T(8,128)S(1)}, u32[]{:S(2)}, u32[]{:S(2)}) collective-permute-start(f32[2,256,128]{2,1,0:T(8,128)S(1)} %get-tuple-element.49), channel_id=1, source_target_pairs={{0,48},{8,56},{16,0},{24,8},{32,16},{40,24},{48,32},{56,40},{64,11... | collective-permute-start | bytes 786440 | tf_op jit(solution)/shard_map/ppermute | solution.py:341
  34.5 8.9 %collective-permute-start.10 = (f32[2,256,128]{2,1,0:T(8,128)S(1)}, f32[2,256,128]{2,1,0:T(8,128)S(1)}, u32[]{:S(2)}, u32[]{:S(2)}) collective-permute-start(f32[2,256,128]{2,1,0:T(8,128)S(1)} %get-tuple-element.50), channel_id=1, source_target_pairs={{0,32},{8,40},{16,48},{24,56},{32,0},{40,8},{48,16},{56,24},{64,96... | collective-permute-start | bytes 786440 | tf_op jit(solution)/shard_map/ppermute | solution.py:341
  43.6 6.7 %collective-permute-start.11 = (f32[4,2,256,128]{3,2,1,0:T(8,128)S(1)}, f32[4,2,256,128]{3,2,1,0:T(8,128)S(1)}, u32[]{:S(2)}, u32[]{:S(2)}) collective-permute-start(f32[4,2,256,128]{3,2,1,0:T(8,128)S(1)} %get-tuple-element.51), channel_id=1, source_target_pairs={{0,8},{8,0},{16,24},{24,16},{32,40},{40,32},{48,56},{56,48},{64,72... | collective-permute-start | bytes 3145736 | tf_op jit(solution)/shard_map/ppermute | solution.py:334
